TPU v7x, 128 devices: a whole 4x4x4 slice. The times are simulated.
128 devices in a mesh: row: 16 (over x, z), col: 8 (over y, core).
Axes of the slice: x: 4, y: 4, z: 4, core: 2. Of those that a mesh axis runs over, the one named last changes fastest.
Arguments:
- tmatrix: bfloat16 [10656, 10656], P('row', 'col'), may hold values from -0.0625 to 0.0625
- panel: bfloat16 [10656, 2048], P('col', 'row'), may hold values from -6 to 6
- contrast: float32 [3, 144, 288], replicated, may hold values from -1.5 to 1.5
Outputs:
- excitation: bfloat16 [10656, 2048], P('col', 'row')
All inputs are finite; a program needn't handle non-finite values.
Results may differ from a plain program's by a relative error of at most 0.006.
Values may be sent and summed in bfloat16 or wider, within the bound.
A program may use at most 128 MiB of HBM per device.

v0:
```python
import jax
import jax.numpy as jnp
import numpy as np
from jax import lax
from jax.sharding import PartitionSpec as P

LDEG = 72
ITERS = 2


def angular_tables(degree):
    lat_count = 2 * degree
    lon_count = 4 * degree
    freq_count = 2 * degree + 1
    colatitude = (np.arange(lat_count) + 0.5) * np.pi / lat_count
    cos_col = np.cos(colatitude)
    sin_col = np.sin(colatitude)
    legendre = np.zeros((freq_count, degree, lat_count))
    diagonal_term = np.full(lat_count, np.sqrt(0.5))
    for order_m in range(degree + 1):
        if order_m > 0:
            diagonal_term = (
                diagonal_term * np.sqrt((2.0 * order_m + 1.0) / (2.0 * order_m)) * sin_col
            )
        earlier = np.zeros(lat_count)
        latest = diagonal_term
        for degree_l in range(order_m, degree + 1):
            if degree_l == order_m:
                current = diagonal_term
            elif degree_l == order_m + 1:
                current = np.sqrt(2.0 * order_m + 3.0) * cos_col * diagonal_term
            else:
                factor_a = np.sqrt((4.0 * degree_l**2 - 1.0) / (degree_l**2 - order_m**2))
                factor_b = np.sqrt(
                    ((degree_l - 1.0) ** 2 - order_m**2) / (4.0 * (degree_l - 1.0) ** 2 - 1.0)
                )
                current = factor_a * (cos_col * latest - factor_b * earlier)
            if degree_l > order_m:
                earlier, latest = (latest, current)
            if degree_l >= 1:
                legendre[order_m, degree_l - 1] = current
                if order_m >= 1:
                    legendre[degree + order_m, degree_l - 1] = current
    longitude = 2.0 * np.pi * np.arange(lon_count) / lon_count
    fourier = np.zeros((freq_count, lon_count))
    fourier[0] = 1.0 / np.sqrt(2.0 * np.pi)
    for order_m in range(1, degree + 1):
        fourier[order_m] = np.cos(order_m * longitude) / np.sqrt(np.pi)
        fourier[degree + order_m] = np.sin(order_m * longitude) / np.sqrt(np.pi)
    weight = sin_col * (np.pi / lat_count) * (2.0 * np.pi / lon_count)
    return (legendre, fourier, weight)


def level_skips(degree):
    skips = []
    for freq_index in range(2 * degree + 1):
        order_m = freq_index if freq_index <= degree else freq_index - degree
        skips.append(max(order_m - 1, 0))
    return skips


def spread_levels(halves, degree):
    columns = halves.shape[2]
    pieces = []
    start = 0
    for skip in level_skips(degree):
        count = degree - skip
        if skip > 0:
            pieces.append(jnp.zeros((2, skip, columns), halves.dtype))
        pieces.append(halves[:, start : start + count, :])
        start = start + count
    return jnp.concatenate(pieces, axis=1).reshape(2, 2 * degree + 1, degree, columns)


def pick_levels(projected, degree):
    pieces = []
    for freq_index, skip in enumerate(level_skips(degree)):
        pieces.append(projected[:, freq_index, skip:, :])
    return jnp.concatenate(pieces, axis=1)


def contrast_apply(coefficients, contrast, degree):
    legendre, fourier, weight = angular_tables(degree)
    legendre_wide = jnp.asarray(legendre, jnp.float32)
    legendre_narrow = jnp.asarray(legendre, jnp.bfloat16)
    fourier = jnp.asarray(fourier, jnp.float32)
    weight = jnp.asarray(weight, jnp.float32)
    columns = coefficients.shape[1]
    halves = coefficients.astype(jnp.bfloat16).reshape(2, -1, columns)
    padded = spread_levels(halves, degree)
    triple = lax.Precision.HIGH
    latitude = jnp.einsum(
        "qlt,cqlk->cktq", legendre_narrow, padded, preferred_element_type=jnp.float32
    )
    surface = jnp.einsum(
        "cktq,qp->cktp", latitude, fourier, precision=triple, preferred_element_type=jnp.float32
    )
    polar = contrast[0] * surface[0] + contrast[1] * surface[1]
    azimuth = contrast[1] * surface[0] + contrast[2] * surface[1]
    weighted = jnp.stack([polar, azimuth]) * weight[:, None]
    spectrum = jnp.einsum(
        "cktp,qp->cktq", weighted, fourier, precision=triple, preferred_element_type=jnp.float32
    )
    projected = jnp.einsum(
        "qlt,cktq->cqlk",
        legendre_wide,
        spectrum,
        precision=triple,
        preferred_element_type=jnp.float32,
    )
    picked = pick_levels(projected, degree)
    return picked.reshape(-1, columns).astype(jnp.bfloat16)


def body(tmatrix, panel, contrast):
    row_count = lax.axis_size("row")
    col_count = lax.axis_size("col")
    per_device = panel.shape[1] // col_count
    local_rows = tmatrix.shape[0]
    current = panel
    for iteration in range(ITERS):
        partial_value = jnp.dot(
            tmatrix,
            lax.all_gather(current, "row", axis=1, tiled=True),
            preferred_element_type=jnp.float32,
        )
        grouped = partial_value.reshape(local_rows, row_count, col_count, per_device)
        regrouped = lax.all_to_all(
            grouped.astype(jnp.bfloat16), "row", split_axis=1, concat_axis=0, tiled=True
        )
        summed = lax.psum_scatter(
            regrouped.astype(jnp.float32).astype(jnp.bfloat16),
            "col",
            scatter_dimension=2,
            tiled=True,
        )
        coupled = contrast_apply(summed.reshape(summed.shape[0], summed.shape[3]), contrast, LDEG)
        full_rows = coupled.shape[0]
        returned = lax.all_to_all(
            coupled.reshape(col_count, full_rows // col_count, 1, per_device),
            "col",
            split_axis=0,
            concat_axis=2,
            tiled=True,
        )
        returned = returned.reshape(full_rows // col_count, col_count * per_device)
        current = (panel.astype(jnp.float32) + returned.astype(jnp.float32)).astype(jnp.bfloat16)
    return current


def solution(mesh):
    placed = (P("row", "col"), P("col", "row"), P())
    return jax.shard_map(
        body, mesh=mesh, in_specs=placed, out_specs=P("col", "row"), check_vma=False
    )
```

profile of v0, /device:TPU:1, one launch (start us, length us, event | category | flops | bytes accessed | tf_op | source)
XLA Modules:
  0.0 546.1 jit_solution(4269901004636810020)
XLA Ops:
  6.5 0.7 all-gather.3.cloned.1.call-update
  7.3 68.5 %all-gather.3.cloned.1.call-done = bf16[1332,2048]{1,0:T(8,128)(2,1)} async-done(((bf16[1332,128]{1,0:T(8,128)(2,1)}), bf16[1332,2048]{1,0:T(8,128)(2,1)}) %all-gather.3.cloned.1.call-update) | async-done | bytes 5455888 | tf_op jit(solution)/shard_map/all_gather | solution.py:124
  75.8 8.5 %convolution_convert_fusion.1 = bf16[666,2048]{1,0:T(8,128)(2,1)} fusion(bf16[666,1332]{1,0:T(8,128)(2,1)S(1)} %copy-done, bf16[1332,2048]{1,0:T(8,128)(2,1)} %all-gather.3.cloned.1.call-done), kind=kOutput, calls=%fused_computation.19 | convolution fusion | flops 3634974720 | bytes 9958032 | tf_op jit(solution)/shard_map/dot_general | solution.py:122
  84.2 4.7 copy.125
  88.9 42.1 %all_to_all.54 = bf16[666,16,8,16]{0,3,2,1:T(8,128)(2,1)S(1)} all-to-all(bf16[666,16,8,16]{0,3,2,1:T(8,128)(2,1)} %bitcast.665), channel_id=1, replica_groups=mesh['row'=16,'col'=8] {'row'}, dimensions={1} | all-to-all | bytes 5455872 | tf_op jit(solution)/shard_map/all_to_all | solution.py:128
  131.0 3.4 copy.126
  134.5 6.9 %all_to_all.43 = bf16[10656,1,8,16]{0,3,2,1:T(8,128)(2,1)} reshape(bf16[16,666,1,8,16]{1,0,4,3,2:T(8,128)(2,1)} %copy.126) | data formatting | bytes 5455872 | tf_op jit(solution)/shard_map/all_to_all | solution.py:128
  141.4 1.1 copy-done.10
  142.4 0.9 slice_bitcast_fusion.2
  143.3 30.5 %reduce-scatter.3.cloned.1.call-done = bf16[10656,1,1,16]{0,3,2,1:T(8,128)(2,1)} async-done(((bf16[10656,1,8,16]{0,3,2,1:T(8,128)(2,1)}), bf16[10656,1,1,16]{0,3,2,1:T(8,128)(2,1)}) %reduce-scatter.3.cloned.1.call-update) | async-done | bytes 341008 | tf_op jit(solution)/shard_map/reduce_scatter | solution.py:131
  173.8 1.3 reshape_reshape.6
  181.1 0.7 fusion.104
  181.8 0.7 fusion.105
  183.9 0.7 fusion.108
  186.7 0.7 fusion.112
  187.4 0.7 fusion.113
  188.1 0.7 fusion.114
  188.8 0.7 fusion.115
  189.5 0.7 fusion.116
  190.2 0.7 fusion.117
  193.6 0.7 fusion.122
  194.3 0.7 fusion.123
  195.0 0.7 fusion.124
  195.7 0.7 fusion.125
  196.4 0.7 fusion.126
  199.2 0.7 fusion.130
  199.9 0.7 fusion.131
  200.6 0.7 fusion.132
  209.8 1.6 concatenate.24
  212.7 11.8 %concatenate.23 = bf16[2,9417,16]{1,0,2:T(2,128)(2,1)S(1)} concatenate(bf16[2,144,16]{1,0,2:T(2,128)(2,1)S(1)} %slice.2639, bf16[2,1,16]{1,0,2:T(2,128)(2,1)S(1)} %broadcast.223, bf16[2,71,16]{1,0,2:T(2,128)(2,1)} %get-tuple-element.457, bf16[2,2,16]{1,0,2:T(2,128)(2,1)S(1)} %broadcast.224, bf16[2,70,16]{1,0,2:T(2,128)(2,1)} %get-tuple-element.455, ...), dimensions={1} | concatenate | bytes 1205376
  224.9 1.5 pad_maximum_fusion
  226.4 3.7 reshape.59
  230.1 3.5 convolution_bitcast_fusion.1
  233.7 7.1 %fusion.8 = f32[2,16,144,288]{3,2,1,0:T(8,128)S(1)} fusion(f32[145,288,1,1]{1,0,3,2:T(8,128)S(1)} %copy-done.2, f32[2,16,144,145]{2,1,0,3:T(8,128)S(1)} %convolution_bitcast_fusion.1), kind=kOutput, calls=%fused_computation.10 | convolution fusion | flops 1154580480 | bytes 8148096 | tf_op jit(solution)/shard_map/cktq,qp->cktp/dot_general | solution.py:95
  240.9 0.7 multiply_add_fusion.3
  241.6 5.6 %fusion = f32[2,16,144,145]{3,2,1,0:T(8,128)} fusion(f32[145,288,1,1]{1,0,3,2:T(8,128)S(1)} %copy-done.2, f32[1,16,144,288]{3,2,1,0:T(8,128)S(1)} %get-tuple-element.8, f32[1,16,144,288]{3,2,1,0:T(8,128)S(1)} %get-tuple-element.7, f32[144]{0:T(256)S(1)} %copy-done.89), kind=kOutput, calls=%fused_computation.1 | convolution fusion | flops 1157234688 | bytes 8148672 | tf_op jit(solution)/shard_map/cktp,qp->cktq/dot_general | solution.py:101
  247.3 6.8 %copy.130 = f32[2,16,144,145]{2,1,0,3:T(8,128)} copy(f32[2,16,144,145]{3,2,1,0:T(8,128)} %fusion) | data formatting | bytes 5345280 | tf_op jit(solution)/shard_map/cktp,qp->cktq/dot_general | solution.py:101
  254.1 9.8 %fusion.13 = bf16[2,145,72,16]{2,3,0,1:T(8,128)(2,1)S(1)} fusion(f32[2,16,144,145]{2,1,0,3:T(8,128)} %copy.130, f32[145,72,144,1]{2,1,3,0:T(8,128)} %constant.13), kind=kOutput, calls=%fused_computation.25 | convolution fusion | flops 288979200 | bytes 9354240 | tf_op jit(solution)/shard_map/qlt,cktq->cqlk/dot_general | solution.py:104
  280.2 1.5 concatenate.17
  282.3 0.8 copy.146
  283.1 7.7 %all-to-all-start.1 = ((bf16[8,1332,1,16]{1,3,2,0:T(8,128)(2,1)}), bf16[8,1332,1,16]{1,3,2,0:T(8,128)(2,1)}, u32[]{:S(2)}, u32[]{:S(2)}) async-start(bf16[8,1332,1,16]{1,3,2,0:T(8,128)(2,1)} %copy.146), calls=%async_computation.2 | async-start | bytes 720896 | tf_op jit(solution)/shard_map/all_to_all | solution.py:139
  290.9 7.6 %all-to-all-done.1 = bf16[8,1332,1,16]{1,3,2,0:T(8,128)(2,1)} async-done(((bf16[8,1332,1,16]{1,3,2,0:T(8,128)(2,1)}), bf16[8,1332,1,16]{1,3,2,0:T(8,128)(2,1)}, u32[]{:S(2)}, u32[]{:S(2)}) %all-to-all-start.1) | async-done | bytes 341024 | tf_op jit(solution)/shard_map/all_to_all | solution.py:139
  298.6 1.0 bitcast_convert_fusion.1
  299.6 0.8 fusion.17
  300.5 58.7 %all-gather.5.cloned.1.call-done = bf16[1332,2048]{0,1:T(8,128)(2,1)} async-done(((bf16[1332,128]{0,1:T(8,128)(2,1)}), bf16[1332,2048]{0,1:T(8,128)(2,1)}) %all-gather.5.cloned.1.call-update) | async-done | bytes 5455888 | tf_op jit(solution)/shard_map/all_gather | solution.py:124
  359.2 8.5 %fusion.12 = bf16[666,2048]{1,0:T(8,128)(2,1)} fusion(bf16[1332,2048]{0,1:T(8,128)(2,1)} %all-gather.5.cloned.1.call-done, bf16[666,1332]{1,0:T(8,128)(2,1)S(1)} %copy-done), kind=kOutput, calls=%fused_computation.20 | convolution fusion | flops 3634974720 | bytes 9958032 | tf_op jit(solution)/shard_map/dot_general | solution.py:122
  367.7 4.7 copy.147
  372.3 43.1 %all_to_all.55 = bf16[666,16,8,16]{0,3,2,1:T(8,128)(2,1)S(1)} all-to-all(bf16[666,16,8,16]{0,3,2,1:T(8,128)(2,1)} %bitcast.667), channel_id=1, replica_groups=mesh['row'=16,'col'=8] {'row'}, dimensions={1} | all-to-all | bytes 5455872 | tf_op jit(solution)/shard_map/all_to_all | solution.py:128
  415.4 3.4 copy.148
  418.8 6.9 %all_to_all.48 = bf16[10656,1,8,16]{0,3,2,1:T(8,128)(2,1)} reshape(bf16[16,666,1,8,16]{1,0,4,3,2:T(8,128)(2,1)} %copy.148) | data formatting | bytes 5455872 | tf_op jit(solution)/shard_map/all_to_all | solution.py:128
  425.7 32.3 %reduce-scatter.5.cloned.1.call-done = bf16[10656,1,1,16]{0,3,2,1:T(8,128)(2,1)} async-done(((bf16[10656,1,8,16]{0,3,2,1:T(8,128)(2,1)}), bf16[10656,1,1,16]{0,3,2,1:T(8,128)(2,1)}) %reduce-scatter.5.cloned.1.call-update) | async-done | bytes 341008 | tf_op jit(solution)/shard_map/reduce_scatter | solution.py:131
  458.0 1.3 reshape_reshape.7
  467.4 1.6 concatenate.21
  469.3 9.9 %concatenate.20 = bf16[2,9417,16]{1,0,2:T(2,128)(2,1)S(1)} concatenate(bf16[2,144,16]{1,0,2:T(2,128)(2,1)S(1)} %slice.2929, bf16[2,1,16]{1,0,2:T(2,128)(2,1)S(1)} %broadcast.223, bf16[2,71,16]{1,0,2:T(2,128)(2,1)S(1)} %get-tuple-element.345, bf16[2,2,16]{1,0,2:T(2,128)(2,1)S(1)} %broadcast.224, bf16[2,70,16]{1,0,2:T(2,128)(2,1)S(1)} %get-tuple-element.343, ...), dimensions={1} | concatenate | bytes 1205376
  479.9 2.0 reshape.60
  482.0 3.5 convolution_bitcast_fusion
  485.5 7.1 %fusion.6 = f32[2,16,144,288]{3,2,1,0:T(8,128)S(1)} fusion(f32[145,288,1,1]{1,0,3,2:T(8,128)S(1)} %copy-done.2, f32[2,16,144,145]{2,1,0,3:T(8,128)S(1)} %convolution_bitcast_fusion), kind=kOutput, calls=%fused_computation.8 | convolution fusion | flops 1154580480 | bytes 8148096 | tf_op jit(solution)/shard_map/cktq,qp->cktp/dot_general | solution.py:95
  492.7 0.7 multiply_add_fusion.1
  493.4 5.9 %fusion.3 = f32[2,16,144,145]{3,2,1,0:T(8,128)} fusion(f32[145,288,1,1]{1,0,3,2:T(8,128)S(1)} %copy-done.2, f32[1,16,144,288]{3,2,1,0:T(8,128)S(1)} %get-tuple-element.6, f32[1,16,144,288]{3,2,1,0:T(8,128)S(1)} %get-tuple-element.5, f32[144]{0:T(256)S(1)} %copy-done.89), kind=kOutput, calls=%fused_computation.5 | convolution fusion | flops 1157234688 | bytes 8148672 | tf_op jit(solution)/shard_map/cktp,qp->cktq/dot_general | solution.py:101
  499.3 6.4 %copy.152 = f32[2,16,144,145]{2,1,0,3:T(8,128)} copy(f32[2,16,144,145]{3,2,1,0:T(8,128)} %fusion.3) | data formatting | bytes 5345280 | tf_op jit(solution)/shard_map/cktp,qp->cktq/dot_general | solution.py:101
  505.7 9.8 %fusion.14 = bf16[2,145,72,16]{2,3,0,1:T(8,128)(2,1)S(1)} fusion(f32[2,16,144,145]{2,1,0,3:T(8,128)} %copy.152, f32[145,72,144,1]{2,1,3,0:T(8,128)} %constant.13), kind=kOutput, calls=%fused_computation.26 | convolution fusion | flops 288979200 | bytes 9354240 | tf_op jit(solution)/shard_map/qlt,cktq->cqlk/dot_general | solution.py:104
  522.3 0.9 concatenate.19
  523.8 13.8 %all_to_all.56 = bf16[8,1332,1,16]{1,3,2,0:T(8,128)(2,1)S(1)} all-to-all(bf16[8,1332,1,16]{1,3,2,0:T(8,128)(2,1)S(1)} %copy.168), channel_id=1, replica_groups=mesh['row'=16,'col'=8] {'col'}, dimensions={0} | all-to-all | bytes 681984 | tf_op jit(solution)/shard_map/all_to_all | solution.py:139
  537.8 0.9 copy.169
  (584 shorter events, 56.7 us)
Async XLA Ops:
  6.5 69.2 %copy-start = (bf16[666,1332]{1,0:T(8,128)(2,1)S(1)}, bf16[666,1332]{1,0:T(8,128)(2,1)}, u32[]{:S(2)}) copy-start(bf16[666,1332]{1,0:T(8,128)(2,1)} %param.11) | copy-start | bytes 5322676
  6.5 69.2 %all-gather.3.cloned.1.call-start = ((), (), s32[]{:S(2)}) async-start(), calls=%async_computation.6 | async-start | bytes 5814272 | tf_op jit(solution)/shard_map/all_gather | solution.py:124
  7.3 166.5 %reduce-scatter.3.cloned.1.call-start = ((), (), s32[]{:S(2)}) async-start(), calls=%async_computation.7 | async-start | bytes 3096576 | tf_op jit(solution)/shard_map/reduce_scatter | solution.py:131
  203.8 20.8 %copy-start.81 = (bf16[2,58,16]{1,0,2:T(2,128)(2,1)}, bf16[2,58,16]{1,0,2:T(2,128)(2,1)S(1)}, u32[]{:S(2)}) copy-start(bf16[2,58,16]{1,0,2:T(2,128)(2,1)S(1)} %broadcast.280) | copy-start | bytes 11140
  203.8 20.7 %copy-start.83 = (bf16[2,59,16]{1,0,2:T(2,128)(2,1)}, bf16[2,59,16]{1,0,2:T(2,128)(2,1)S(1)}, u32[]{:S(2)}) copy-start(bf16[2,59,16]{1,0,2:T(2,128)(2,1)S(1)} %broadcast.281) | copy-start | bytes 11332
  203.8 20.7 %copy-start.85 = (bf16[2,60,16]{1,0,2:T(2,128)(2,1)}, bf16[2,60,16]{1,0,2:T(2,128)(2,1)S(1)}, u32[]{:S(2)}) copy-start(bf16[2,60,16]{1,0,2:T(2,128)(2,1)S(1)} %broadcast.282) | copy-start | bytes 11524
  203.8 20.7 %copy-start.87 = (bf16[2,61,16]{1,0,2:T(2,128)(2,1)}, bf16[2,61,16]{1,0,2:T(2,128)(2,1)S(1)}, u32[]{:S(2)}) copy-start(bf16[2,61,16]{1,0,2:T(2,128)(2,1)S(1)} %broadcast.283) | copy-start | bytes 11716
  211.8 12.7 %copy-start.11 = (bf16[2,23,16]{1,0,2:T(2,128)(2,1)}, bf16[2,23,16]{1,0,2:T(2,128)(2,1)S(1)}, u32[]{:S(2)}) copy-start(bf16[2,23,16]{1,0,2:T(2,128)(2,1)S(1)} %broadcast.245) | copy-start | bytes 4420
  211.8 12.7 %copy-start.13 = (bf16[2,24,16]{1,0,2:T(2,128)(2,1)}, bf16[2,24,16]{1,0,2:T(2,128)(2,1)S(1)}, u32[]{:S(2)}) copy-start(bf16[2,24,16]{1,0,2:T(2,128)(2,1)S(1)} %broadcast.246) | copy-start | bytes 4612
  211.9 12.7 %copy-start.15 = (bf16[2,25,16]{1,0,2:T(2,128)(2,1)}, bf16[2,25,16]{1,0,2:T(2,128)(2,1)S(1)}, u32[]{:S(2)}) copy-start(bf16[2,25,16]{1,0,2:T(2,128)(2,1)S(1)} %broadcast.247) | copy-start | bytes 4804
  211.9 12.7 %copy-start.17 = (bf16[2,26,16]{1,0,2:T(2,128)(2,1)}, bf16[2,26,16]{1,0,2:T(2,128)(2,1)S(1)}, u32[]{:S(2)}) copy-start(bf16[2,26,16]{1,0,2:T(2,128)(2,1)S(1)} %broadcast.248) | copy-start | bytes 4996
  211.9 12.7 %copy-start.19 = (bf16[2,27,16]{1,0,2:T(2,128)(2,1)}, bf16[2,27,16]{1,0,2:T(2,128)(2,1)S(1)}, u32[]{:S(2)}) copy-start(bf16[2,27,16]{1,0,2:T(2,128)(2,1)S(1)} %broadcast.249) | copy-start | bytes 5188
  211.9 12.7 %copy-start.21 = (bf16[2,28,16]{1,0,2:T(2,128)(2,1)}, bf16[2,28,16]{1,0,2:T(2,128)(2,1)S(1)}, u32[]{:S(2)}) copy-start(bf16[2,28,16]{1,0,2:T(2,128)(2,1)S(1)} %broadcast.250) | copy-start | bytes 5380
  211.9 12.7 %copy-start.23 = (bf16[2,29,16]{1,0,2:T(2,128)(2,1)}, bf16[2,29,16]{1,0,2:T(2,128)(2,1)S(1)}, u32[]{:S(2)}) copy-start(bf16[2,29,16]{1,0,2:T(2,128)(2,1)S(1)} %broadcast.251) | copy-start | bytes 5572
  212.0 12.6 %copy-start.25 = (bf16[2,30,16]{1,0,2:T(2,128)(2,1)}, bf16[2,30,16]{1,0,2:T(2,128)(2,1)S(1)}, u32[]{:S(2)}) copy-start(bf16[2,30,16]{1,0,2:T(2,128)(2,1)S(1)} %broadcast.252) | copy-start | bytes 5764
  212.0 12.6 %copy-start.27 = (bf16[2,31,16]{1,0,2:T(2,128)(2,1)}, bf16[2,31,16]{1,0,2:T(2,128)(2,1)S(1)}, u32[]{:S(2)}) copy-start(bf16[2,31,16]{1,0,2:T(2,128)(2,1)S(1)} %broadcast.253) | copy-start | bytes 5956
  212.0 12.6 %copy-start.29 = (bf16[2,32,16]{1,0,2:T(2,128)(2,1)}, bf16[2,32,16]{1,0,2:T(2,128)(2,1)S(1)}, u32[]{:S(2)}) copy-start(bf16[2,32,16]{1,0,2:T(2,128)(2,1)S(1)} %broadcast.254) | copy-start | bytes 6148
  212.0 12.6 %copy-start.31 = (bf16[2,33,16]{1,0,2:T(2,128)(2,1)}, bf16[2,33,16]{1,0,2:T(2,128)(2,1)S(1)}, u32[]{:S(2)}) copy-start(bf16[2,33,16]{1,0,2:T(2,128)(2,1)S(1)} %broadcast.255) | copy-start | bytes 6340
  212.1 12.6 %copy-start.33 = (bf16[2,34,16]{1,0,2:T(2,128)(2,1)}, bf16[2,34,16]{1,0,2:T(2,128)(2,1)S(1)}, u32[]{:S(2)}) copy-start(bf16[2,34,16]{1,0,2:T(2,128)(2,1)S(1)} %broadcast.256) | copy-start | bytes 6532
  212.1 12.6 %copy-start.35 = (bf16[2,35,16]{1,0,2:T(2,128)(2,1)}, bf16[2,35,16]{1,0,2:T(2,128)(2,1)S(1)}, u32[]{:S(2)}) copy-start(bf16[2,35,16]{1,0,2:T(2,128)(2,1)S(1)} %broadcast.257) | copy-start | bytes 6724
  212.1 12.6 %copy-start.37 = (bf16[2,36,16]{1,0,2:T(2,128)(2,1)}, bf16[2,36,16]{1,0,2:T(2,128)(2,1)S(1)}, u32[]{:S(2)}) copy-start(bf16[2,36,16]{1,0,2:T(2,128)(2,1)S(1)} %broadcast.258) | copy-start | bytes 6916
  212.1 12.5 %copy-start.39 = (bf16[2,37,16]{1,0,2:T(2,128)(2,1)}, bf16[2,37,16]{1,0,2:T(2,128)(2,1)S(1)}, u32[]{:S(2)}) copy-start(bf16[2,37,16]{1,0,2:T(2,128)(2,1)S(1)} %broadcast.259) | copy-start | bytes 7108
  212.2 12.5 %copy-start.41 = (bf16[2,38,16]{1,0,2:T(2,128)(2,1)}, bf16[2,38,16]{1,0,2:T(2,128)(2,1)S(1)}, u32[]{:S(2)}) copy-start(bf16[2,38,16]{1,0,2:T(2,128)(2,1)S(1)} %broadcast.260) | copy-start | bytes 7300
  212.2 12.5 %copy-start.43 = (bf16[2,39,16]{1,0,2:T(2,128)(2,1)}, bf16[2,39,16]{1,0,2:T(2,128)(2,1)S(1)}, u32[]{:S(2)}) copy-start(bf16[2,39,16]{1,0,2:T(2,128)(2,1)S(1)} %broadcast.261) | copy-start | bytes 7492
  212.2 12.5 %copy-start.45 = (bf16[2,40,16]{1,0,2:T(2,128)(2,1)}, bf16[2,40,16]{1,0,2:T(2,128)(2,1)S(1)}, u32[]{:S(2)}) copy-start(bf16[2,40,16]{1,0,2:T(2,128)(2,1)S(1)} %broadcast.262) | copy-start | bytes 7684
  212.2 12.5 %copy-start.47 = (bf16[2,41,16]{1,0,2:T(2,128)(2,1)}, bf16[2,41,16]{1,0,2:T(2,128)(2,1)S(1)}, u32[]{:S(2)}) copy-start(bf16[2,41,16]{1,0,2:T(2,128)(2,1)S(1)} %broadcast.263) | copy-start | bytes 7876
  212.3 12.5 %copy-start.49 = (bf16[2,42,16]{1,0,2:T(2,128)(2,1)}, bf16[2,42,16]{1,0,2:T(2,128)(2,1)S(1)}, u32[]{:S(2)}) copy-start(bf16[2,42,16]{1,0,2:T(2,128)(2,1)S(1)} %broadcast.264) | copy-start | bytes 8068
  212.3 12.5 %copy-start.51 = (bf16[2,43,16]{1,0,2:T(2,128)(2,1)}, bf16[2,43,16]{1,0,2:T(2,128)(2,1)S(1)}, u32[]{:S(2)}) copy-start(bf16[2,43,16]{1,0,2:T(2,128)(2,1)S(1)} %broadcast.265) | copy-start | bytes 8260
  212.3 12.4 %copy-start.53 = (bf16[2,44,16]{1,0,2:T(2,128)(2,1)}, bf16[2,44,16]{1,0,2:T(2,128)(2,1)S(1)}, u32[]{:S(2)}) copy-start(bf16[2,44,16]{1,0,2:T(2,128)(2,1)S(1)} %broadcast.266) | copy-start | bytes 8452
  212.3 12.4 %copy-start.55 = (bf16[2,45,16]{1,0,2:T(2,128)(2,1)}, bf16[2,45,16]{1,0,2:T(2,128)(2,1)S(1)}, u32[]{:S(2)}) copy-start(bf16[2,45,16]{1,0,2:T(2,128)(2,1)S(1)} %broadcast.267) | copy-start | bytes 8644
  212.4 12.4 %copy-start.57 = (bf16[2,46,16]{1,0,2:T(2,128)(2,1)}, bf16[2,46,16]{1,0,2:T(2,128)(2,1)S(1)}, u32[]{:S(2)}) copy-start(bf16[2,46,16]{1,0,2:T(2,128)(2,1)S(1)} %broadcast.268) | copy-start | bytes 8836
  212.4 12.4 %copy-start.59 = (bf16[2,47,16]{1,0,2:T(2,128)(2,1)}, bf16[2,47,16]{1,0,2:T(2,128)(2,1)S(1)}, u32[]{:S(2)}) copy-start(bf16[2,47,16]{1,0,2:T(2,128)(2,1)S(1)} %broadcast.269) | copy-start | bytes 9028
  212.4 12.4 %copy-start.61 = (bf16[2,48,16]{1,0,2:T(2,128)(2,1)}, bf16[2,48,16]{1,0,2:T(2,128)(2,1)S(1)}, u32[]{:S(2)}) copy-start(bf16[2,48,16]{1,0,2:T(2,128)(2,1)S(1)} %broadcast.270) | copy-start | bytes 9220
  212.4 12.4 %copy-start.63 = (bf16[2,49,16]{1,0,2:T(2,128)(2,1)}, bf16[2,49,16]{1,0,2:T(2,128)(2,1)S(1)}, u32[]{:S(2)}) copy-start(bf16[2,49,16]{1,0,2:T(2,128)(2,1)S(1)} %broadcast.271) | copy-start | bytes 9412
  212.5 12.3 %copy-start.65 = (bf16[2,50,16]{1,0,2:T(2,128)(2,1)}, bf16[2,50,16]{1,0,2:T(2,128)(2,1)S(1)}, u32[]{:S(2)}) copy-start(bf16[2,50,16]{1,0,2:T(2,128)(2,1)S(1)} %broadcast.272) | copy-start | bytes 9604
  212.5 12.3 %copy-start.67 = (bf16[2,51,16]{1,0,2:T(2,128)(2,1)}, bf16[2,51,16]{1,0,2:T(2,128)(2,1)S(1)}, u32[]{:S(2)}) copy-start(bf16[2,51,16]{1,0,2:T(2,128)(2,1)S(1)} %broadcast.273) | copy-start | bytes 9796
  212.5 12.3 %copy-start.69 = (bf16[2,52,16]{1,0,2:T(2,128)(2,1)}, bf16[2,52,16]{1,0,2:T(2,128)(2,1)S(1)}, u32[]{:S(2)}) copy-start(bf16[2,52,16]{1,0,2:T(2,128)(2,1)S(1)} %broadcast.274) | copy-start | bytes 9988
  212.5 12.3 %copy-start.71 = (bf16[2,53,16]{1,0,2:T(2,128)(2,1)}, bf16[2,53,16]{1,0,2:T(2,128)(2,1)S(1)}, u32[]{:S(2)}) copy-start(bf16[2,53,16]{1,0,2:T(2,128)(2,1)S(1)} %broadcast.275) | copy-start | bytes 10180
  212.6 12.3 %copy-start.73 = (bf16[2,54,16]{1,0,2:T(2,128)(2,1)}, bf16[2,54,16]{1,0,2:T(2,128)(2,1)S(1)}, u32[]{:S(2)}) copy-start(bf16[2,54,16]{1,0,2:T(2,128)(2,1)S(1)} %broadcast.276) | copy-start | bytes 10372
  212.6 12.3 %copy-start.75 = (bf16[2,55,16]{1,0,2:T(2,128)(2,1)}, bf16[2,55,16]{1,0,2:T(2,128)(2,1)S(1)}, u32[]{:S(2)}) copy-start(bf16[2,55,16]{1,0,2:T(2,128)(2,1)S(1)} %broadcast.277) | copy-start | bytes 10564
  212.6 12.3 %copy-start.77 = (bf16[2,56,16]{1,0,2:T(2,128)(2,1)}, bf16[2,56,16]{1,0,2:T(2,128)(2,1)S(1)}, u32[]{:S(2)}) copy-start(bf16[2,56,16]{1,0,2:T(2,128)(2,1)S(1)} %broadcast.278) | copy-start | bytes 10756
  212.6 12.2 %copy-start.79 = (bf16[2,57,16]{1,0,2:T(2,128)(2,1)}, bf16[2,57,16]{1,0,2:T(2,128)(2,1)S(1)}, u32[]{:S(2)}) copy-start(bf16[2,57,16]{1,0,2:T(2,128)(2,1)S(1)} %broadcast.279) | copy-start | bytes 10948
  281.9 8.8 %copy-start.9 = (bf16[1332,128]{1,0:T(8,128)(2,1)S(1)}, bf16[1332,128]{1,0:T(8,128)(2,1)}, u32[]{:S(2)}) copy-start(bf16[1332,128]{1,0:T(8,128)(2,1)} %param.12) | copy-start | bytes 1022980
  283.1 15.5 %all-to-all-start.1 = ((bf16[8,1332,1,16]{1,3,2,0:T(8,128)(2,1)}), bf16[8,1332,1,16]{1,3,2,0:T(8,128)(2,1)}, u32[]{:S(2)}, u32[]{:S(2)}) async-start(bf16[8,1332,1,16]{1,3,2,0:T(8,128)(2,1)} %copy.146), calls=%async_computation.2 | async-start | bytes 720896 | tf_op jit(solution)/shard_map/all_to_all | solution.py:139
  290.7 68.5 %all-gather.5.cloned.1.call-start = ((), (), s32[]{:S(2)}) async-start(), calls=%async_computation.8 | async-start | bytes 6127616 | tf_op jit(solution)/shard_map/all_gather | solution.py:124
  300.4 157.6 %reduce-scatter.5.cloned.1.call-start = ((), (), s32[]{:S(2)}) async-start(), calls=%async_computation.9 | async-start | bytes 3096576 | tf_op jit(solution)/shard_map/reduce_scatter | solution.py:131
  460.7 8.3 %copy-start.12 = (bf16[2,23,16]{1,0,2:T(2,128)(2,1)S(1)}, bf16[2,23,16]{1,0,2:T(2,128)(2,1)}, u32[]{:S(2)}) copy-start(bf16[2,23,16]{1,0,2:T(2,128)(2,1)} %copy-done.11) | copy-start | bytes 4420
  460.8 8.3 %copy-start.14 = (bf16[2,24,16]{1,0,2:T(2,128)(2,1)S(1)}, bf16[2,24,16]{1,0,2:T(2,128)(2,1)}, u32[]{:S(2)}) copy-start(bf16[2,24,16]{1,0,2:T(2,128)(2,1)} %copy-done.13) | copy-start | bytes 4612
  460.8 8.3 %copy-start.16 = (bf16[2,25,16]{1,0,2:T(2,128)(2,1)S(1)}, bf16[2,25,16]{1,0,2:T(2,128)(2,1)}, u32[]{:S(2)}) copy-start(bf16[2,25,16]{1,0,2:T(2,128)(2,1)} %copy-done.15) | copy-start | bytes 4804
  460.8 8.3 %copy-start.18 = (bf16[2,26,16]{1,0,2:T(2,128)(2,1)S(1)}, bf16[2,26,16]{1,0,2:T(2,128)(2,1)}, u32[]{:S(2)}) copy-start(bf16[2,26,16]{1,0,2:T(2,128)(2,1)} %copy-done.17) | copy-start | bytes 4996
  460.8 8.3 %copy-start.20 = (bf16[2,27,16]{1,0,2:T(2,128)(2,1)S(1)}, bf16[2,27,16]{1,0,2:T(2,128)(2,1)}, u32[]{:S(2)}) copy-start(bf16[2,27,16]{1,0,2:T(2,128)(2,1)} %copy-done.19) | copy-start | bytes 5188
  460.8 8.3 %copy-start.22 = (bf16[2,28,16]{1,0,2:T(2,128)(2,1)S(1)}, bf16[2,28,16]{1,0,2:T(2,128)(2,1)}, u32[]{:S(2)}) copy-start(bf16[2,28,16]{1,0,2:T(2,128)(2,1)} %copy-done.21) | copy-start | bytes 5380
  460.8 8.3 %copy-start.24 = (bf16[2,29,16]{1,0,2:T(2,128)(2,1)S(1)}, bf16[2,29,16]{1,0,2:T(2,128)(2,1)}, u32[]{:S(2)}) copy-start(bf16[2,29,16]{1,0,2:T(2,128)(2,1)} %copy-done.23) | copy-start | bytes 5572
  460.8 8.3 %copy-start.26 = (bf16[2,30,16]{1,0,2:T(2,128)(2,1)S(1)}, bf16[2,30,16]{1,0,2:T(2,128)(2,1)}, u32[]{:S(2)}) copy-start(bf16[2,30,16]{1,0,2:T(2,128)(2,1)} %copy-done.25) | copy-start | bytes 5764
  460.8 8.3 %copy-start.28 = (bf16[2,31,16]{1,0,2:T(2,128)(2,1)S(1)}, bf16[2,31,16]{1,0,2:T(2,128)(2,1)}, u32[]{:S(2)}) copy-start(bf16[2,31,16]{1,0,2:T(2,128)(2,1)} %copy-done.27) | copy-start | bytes 5956
  460.8 8.3 %copy-start.30 = (bf16[2,32,16]{1,0,2:T(2,128)(2,1)S(1)}, bf16[2,32,16]{1,0,2:T(2,128)(2,1)}, u32[]{:S(2)}) copy-start(bf16[2,32,16]{1,0,2:T(2,128)(2,1)} %copy-done.29) | copy-start | bytes 6148
  460.8 8.3 %copy-start.32 = (bf16[2,33,16]{1,0,2:T(2,128)(2,1)S(1)}, bf16[2,33,16]{1,0,2:T(2,128)(2,1)}, u32[]{:S(2)}) copy-start(bf16[2,33,16]{1,0,2:T(2,128)(2,1)} %copy-done.31) | copy-start | bytes 6340
  460.9 8.3 %copy-start.34 = (bf16[2,34,16]{1,0,2:T(2,128)(2,1)S(1)}, bf16[2,34,16]{1,0,2:T(2,128)(2,1)}, u32[]{:S(2)}) copy-start(bf16[2,34,16]{1,0,2:T(2,128)(2,1)} %copy-done.33) | copy-start | bytes 6532
  460.9 8.3 %copy-start.36 = (bf16[2,35,16]{1,0,2:T(2,128)(2,1)S(1)}, bf16[2,35,16]{1,0,2:T(2,128)(2,1)}, u32[]{:S(2)}) copy-start(bf16[2,35,16]{1,0,2:T(2,128)(2,1)} %copy-done.35) | copy-start | bytes 6724
  460.9 8.3 %copy-start.38 = (bf16[2,36,16]{1,0,2:T(2,128)(2,1)S(1)}, bf16[2,36,16]{1,0,2:T(2,128)(2,1)}, u32[]{:S(2)}) copy-start(bf16[2,36,16]{1,0,2:T(2,128)(2,1)} %copy-done.37) | copy-start | bytes 6916
  460.9 8.3 %copy-start.40 = (bf16[2,37,16]{1,0,2:T(2,128)(2,1)S(1)}, bf16[2,37,16]{1,0,2:T(2,128)(2,1)}, u32[]{:S(2)}) copy-start(bf16[2,37,16]{1,0,2:T(2,128)(2,1)} %copy-done.39) | copy-start | bytes 7108
  460.9 8.3 %copy-start.42 = (bf16[2,38,16]{1,0,2:T(2,128)(2,1)S(1)}, bf16[2,38,16]{1,0,2:T(2,128)(2,1)}, u32[]{:S(2)}) copy-start(bf16[2,38,16]{1,0,2:T(2,128)(2,1)} %copy-done.41) | copy-start | bytes 7300
  460.9 8.3 %copy-start.44 = (bf16[2,39,16]{1,0,2:T(2,128)(2,1)S(1)}, bf16[2,39,16]{1,0,2:T(2,128)(2,1)}, u32[]{:S(2)}) copy-start(bf16[2,39,16]{1,0,2:T(2,128)(2,1)} %copy-done.43) | copy-start | bytes 7492
  460.9 8.3 %copy-start.46 = (bf16[2,40,16]{1,0,2:T(2,128)(2,1)S(1)}, bf16[2,40,16]{1,0,2:T(2,128)(2,1)}, u32[]{:S(2)}) copy-start(bf16[2,40,16]{1,0,2:T(2,128)(2,1)} %copy-done.45) | copy-start | bytes 7684
  (31 other events, 222.3 us)
Sparse Core Ops, SparseCore 0:
  9.5 66.2 all-gather.2
  141.5 32.2 reduce-scatter.2
  300.5 58.5 all-gather.4
  425.8 32.1 reduce-scatter.4
where the time goes:
time: 550 us; the launch traced here: 546 us
  waiting for transfers between devices  198 us (36%)
  local copies, waits for them, and re-layouts  150 us (27%)
  blocking collectives  99 us (18%)
  matrix products  69.4 us (13%)
  between operations  15.9 us (3%)
  starting transfers between devices  7.75 us (1%)
  other arithmetic  5.58 us (1%)
    all_gather x2, waiting for transfers between devices, body(): lax.all_gather(current, 'row', axis=1, tiled=True)  127 us
    all_to_all x2, blocking collectives, body(): lax.all_to_all(grouped.astype(jnp.bfloat16), 'row', split_axis=1, concat_...  85.2 us
    reduce_scatter x2, waiting for transfers between devices, body(): lax.psum_scatter(regrouped.astype(jnp.float32).astype(jnp.bfloat16), 'col...  62.8 us
    slice x174, local copies, waits for them, and re-layouts, spread_levels(): pieces.append(halves[:, start:start + count, :])  35.8 us
    unnamed x185, local copies, waits for them, and re-layouts  27.3 us
    squeeze x161, local copies, waits for them, and re-layouts, pick_levels(): pieces.append(projected[:, freq_index, skip:, :])  22.9 us
    all_to_all x4, local copies, waits for them, and re-layouts, body(): lax.all_to_all(grouped.astype(jnp.bfloat16), 'row', split_axis=1, concat_...  20.6 us
    dot_general x2, matrix products, contrast_apply(): jnp.einsum('qlt,cktq->cqlk', legendre_wide, spectrum, precision=triple, p...  19.7 us
  transfers between devices with their start and end apart: 5, of which 5 were waited for; matrix products, arithmetic and copies ran while one was open for 0% of the time, Pallas kernels for 0%

commit v1 on v0

--- a/solution.py
+++ b/solution.py
@@ -119,10 +119,16 @@
     local_rows = tmatrix.shape[0]
     current = panel
     for iteration in range(ITERS):
+
+        def shape_columns(w_in, a_name):
+            z_new = jnp.concatenate(
+                lax.all_to_all(jnp.stack([w_in] * lax.axis_size(a_name), axis=0), a_name, 0, 0),
+                axis=1,
+            )
+            return z_new
+
         partial_value = jnp.dot(
-            tmatrix,
-            lax.all_gather(current, "row", axis=1, tiled=True),
-            preferred_element_type=jnp.float32,
+            tmatrix, shape_columns(current, a_name="row"), preferred_element_type=jnp.float32
         )
         grouped = partial_value.reshape(local_rows, row_count, col_count, per_device)
         regrouped = lax.all_to_all(

time: 550 us -> 627 us (1.14)
  blocking collectives: 99 us -> 238 us
  waiting for transfers between devices: 198 us -> 70.3 us
  local copies, waits for them, and re-layouts: 150 us -> 215 us
    all_to_all x0 -> x2, blocking collectives: none -> 141 us  [shape_columns(): lax.all_to_all(jnp.stack([w_in] * lax.axis_size(a_name), axis=0), a_name,...]
    all_gather x2 -> x0, waiting for transfers between devices: 127 us -> none  [body(): lax.all_gather(current, 'row', axis=1, tiled=True)]
    slice x174, local copies, waits for them, and re-layouts: 35.8 us -> 65.1 us  [spread_levels(): pieces.append(halves[:, start:start + count, :])]
    reshape x0 -> x2, local copies, waits for them, and re-layouts: none -> 14.7 us  [shape_columns(): jnp.concatenate(lax.all_to_all(jnp.stack([w_in] * lax.axis_size(a_name),...]
    unnamed x185 -> x191, local copies, waits for them, and re-layouts: 27.3 us -> 39.6 us
    dot_general x0 -> x1, local copies, waits for them, and re-layouts: none -> 8.14 us  [body(): jnp.dot(tmatrix, shape_columns(current, a_name='row'), preferred_element_...]
  transfers between devices with their start and end apart: 5 -> 3, of which waited for: 5 -> 3; matrix products, arithmetic and copies ran while one was open for 0% -> 0% of each run, Pallas kernels for 0% -> 0%
where the time goes in v1:
time: 627 us; the launch traced here: 620 us
  blocking collectives  238 us (38%)
  local copies, waits for them, and re-layouts  215 us (34%)
  waiting for transfers between devices  70.3 us (11%)
  matrix products  66.3 us (11%)
  between operations  16 us (3%)
  starting transfers between devices  7.52 us (1%)
  other arithmetic  6.51 us (1%)
    all_to_all x2, blocking collectives, shape_columns(): lax.all_to_all(jnp.stack([w_in] * lax.axis_size(a_name), axis=0), a_name,...  141 us
    all_to_all x2, blocking collectives, body(): lax.all_to_all(grouped.astype(jnp.bfloat16), 'row', split_axis=1, concat_...  82.5 us
    slice x174, local copies, waits for them, and re-layouts, spread_levels(): pieces.append(halves[:, start:start + count, :])  65.1 us
    reduce_scatter x2, waiting for transfers between devices, body(): lax.psum_scatter(regrouped.astype(jnp.float32).astype(jnp.bfloat16), 'col...  62.7 us
    unnamed x191, local copies, waits for them, and re-layouts  39.6 us
    squeeze x161, local copies, waits for them, and re-layouts, pick_levels(): pieces.append(projected[:, freq_index, skip:, :])  23 us
    all_to_all x4, local copies, waits for them, and re-layouts, body(): lax.all_to_all(grouped.astype(jnp.bfloat16), 'row', split_axis=1, concat_...  20.5 us
    dot_general x2, matrix products, contrast_apply(): jnp.einsum('qlt,cktq->cqlk', legendre_wide, spectrum, precision=triple, p...  19.7 us
  transfers between devices with their start and end apart: 3, of which 3 were waited for; matrix products, arithmetic and copies ran while one was open for 0% of the time, Pallas kernels for 0%

profile of v1, /device:TPU:1, one launch (start us, length us, event | category | flops | bytes accessed | tf_op | source)
XLA Modules:
  0.0 619.8 jit_solution(7573031915973509975)
XLA Ops:
  6.5 1.8 stack.8
  8.4 72.0 %all_to_all.64 = bf16[16,1332,128]{2,1,0:T(8,128)(2,1)S(1)} all-to-all(bf16[16,1332,128]{2,1,0:T(8,128)(2,1)S(1)} %stack.8), channel_id=1, replica_groups=mesh['row'=16,'col'=8] {'row'}, dimensions={0} | all-to-all | bytes 10911744 | tf_op jit(solution)/shard_map/all_to_all | solution.py:125
  80.4 7.4 %copy.175 = bf16[1332,16,128]{2,1,0:T(8,128)(2,1)S(1)} copy(bf16[1332,16,128]{2,0,1:T(8,128)(2,1)S(1)} %bitcast.680) | data formatting | bytes 10911744 | tf_op jit(solution)/shard_map/reshape | solution.py:124
  87.7 1.0 pad.8
  88.8 5.1 copy.243
  93.9 8.1 %copy.176 = bf16[2048,1332]{1,0:T(8,128)(2,1)} copy(bf16[2048,1332]{0,1:T(8,128)(2,1)} %bitcast.682) | data formatting | bytes 10911744 | tf_op jit(solution)/shard_map/dot_general | solution.py:130
  102.0 8.2 %convolution_convert_fusion.1 = bf16[666,16,8,16]{0,3,2,1:T(8,128)(2,1)S(1)} fusion(bf16[16,8,16,1332]{3,2,1,0:T(8,128)(2,1)} %bitcast.687, bf16[666,1332]{1,0:T(8,128)(2,1)S(1)} %copy-done), kind=kOutput, calls=%fused_computation.22 | convolution fusion | flops 3634974720 | bytes 9958032 | tf_op jit(solution)/shard_map/dot_general | solution.py:130
  110.2 40.4 %all_to_all.65 = bf16[666,16,8,16]{0,3,2,1:T(8,128)(2,1)S(1)} all-to-all(bf16[666,16,8,16]{0,3,2,1:T(8,128)(2,1)S(1)} %convolution_convert_fusion.1), channel_id=1, replica_groups=mesh['row'=16,'col'=8] {'row'}, dimensions={1} | all-to-all | bytes 5455872 | tf_op jit(solution)/shard_map/all_to_all | solution.py:134
  150.6 3.4 copy.177
  154.0 6.9 %all_to_all.50 = bf16[10656,1,8,16]{0,3,2,1:T(8,128)(2,1)} reshape(bf16[16,666,1,8,16]{1,0,4,3,2:T(8,128)(2,1)} %copy.177) | data formatting | bytes 5455872 | tf_op jit(solution)/shard_map/all_to_all | solution.py:134
  160.9 1.1 copy-done.11
  162.0 0.9 slice_bitcast_fusion.2
  162.9 31.9 %reduce-scatter.3.cloned.1.call-done = bf16[10656,1,1,16]{0,3,2,1:T(8,128)(2,1)} async-done(((bf16[10656,1,8,16]{0,3,2,1:T(8,128)(2,1)}), bf16[10656,1,1,16]{0,3,2,1:T(8,128)(2,1)}) %reduce-scatter.3.cloned.1.call-update) | async-done | bytes 341008 | tf_op jit(solution)/shard_map/reduce_scatter | solution.py:137
  194.7 1.3 reshape_reshape.6
  202.8 0.7 fusion.106
  206.9 0.7 fusion.112
  212.5 0.7 fusion.120
  218.7 0.7 fusion.129
  230.7 1.6 concatenate.24
  233.5 11.8 %concatenate.23 = bf16[2,9417,16]{1,0,2:T(2,128)(2,1)S(1)} concatenate(bf16[2,144,16]{1,0,2:T(2,128)(2,1)S(1)} %slice.2639, bf16[2,1,16]{1,0,2:T(2,128)(2,1)S(1)} %broadcast.227, bf16[2,71,16]{1,0,2:T(2,128)(2,1)} %get-tuple-element.457, bf16[2,2,16]{1,0,2:T(2,128)(2,1)S(1)} %broadcast.228, bf16[2,70,16]{1,0,2:T(2,128)(2,1)} %get-tuple-element.455, ...), dimensions={1} | concatenate | bytes 1205376
  245.7 1.5 pad_maximum_fusion
  247.2 3.9 reshape.80
  251.2 3.6 convolution_bitcast_fusion.1
  254.8 7.1 %fusion.8 = f32[2,16,144,288]{3,2,1,0:T(8,128)S(1)} fusion(f32[145,288,1,1]{1,0,3,2:T(8,128)S(1)} %copy-done.1, f32[2,16,144,145]{2,1,0,3:T(8,128)S(1)} %convolution_bitcast_fusion.1), kind=kOutput, calls=%fused_computation.10 | convolution fusion | flops 1154580480 | bytes 8148096 | tf_op jit(solution)/shard_map/cktq,qp->cktp/dot_general | solution.py:95
  261.9 0.7 multiply_add_fusion.3
  262.7 5.6 fusion
  268.3 6.5 %copy.181 = f32[2,16,144,145]{2,1,0,3:T(8,128)} copy(f32[2,16,144,145]{3,2,1,0:T(8,128)} %fusion) | data formatting | bytes 5345280 | tf_op jit(solution)/shard_map/cktp,qp->cktq/dot_general | solution.py:101
  274.8 9.8 %fusion.14 = bf16[2,145,72,16]{2,3,0,1:T(8,128)(2,1)S(1)} fusion(f32[2,16,144,145]{2,1,0,3:T(8,128)} %copy.181, f32[145,72,144,1]{2,1,3,0:T(8,128)} %constant.13), kind=kOutput, calls=%fused_computation.26 | convolution fusion | flops 288979200 | bytes 9354240 | tf_op jit(solution)/shard_map/qlt,cktq->cqlk/dot_general | solution.py:104
  301.0 1.5 concatenate.17
  303.1 0.8 copy.197
  303.9 7.5 %all-to-all-start.2 = ((bf16[8,1332,1,16]{1,3,2,0:T(8,128)(2,1)}), bf16[8,1332,1,16]{1,3,2,0:T(8,128)(2,1)}, u32[]{:S(2)}, u32[]{:S(2)}) async-start(bf16[8,1332,1,16]{1,3,2,0:T(8,128)(2,1)} %copy.197), calls=%async_computation.3 | async-start | bytes 720896 | tf_op jit(solution)/shard_map/all_to_all | solution.py:145
  311.7 7.6 %all-to-all-done.2 = bf16[8,1332,1,16]{1,3,2,0:T(8,128)(2,1)} async-done(((bf16[8,1332,1,16]{1,3,2,0:T(8,128)(2,1)}), bf16[8,1332,1,16]{1,3,2,0:T(8,128)(2,1)}, u32[]{:S(2)}, u32[]{:S(2)}) %all-to-all-start.2) | async-done | bytes 341024 | tf_op jit(solution)/shard_map/all_to_all | solution.py:145
  319.3 1.0 bitcast_convert_fusion.1
  320.3 0.8 fusion.18
  321.1 1.2 copy.198
  322.3 0.7 stack.10
  323.1 69.2 %all_to_all.66 = bf16[16,1332,128]{2,1,0:T(8,128)(2,1)S(1)} all-to-all(bf16[16,1332,128]{2,1,0:T(8,128)(2,1)S(1)} %stack.10), channel_id=1, replica_groups=mesh['row'=16,'col'=8] {'row'}, dimensions={0} | all-to-all | bytes 10911744 | tf_op jit(solution)/shard_map/all_to_all | solution.py:125
  392.3 7.4 %copy.199 = bf16[1332,16,128]{2,1,0:T(8,128)(2,1)S(1)} copy(bf16[1332,16,128]{2,0,1:T(8,128)(2,1)S(1)} %bitcast.683) | data formatting | bytes 10911744 | tf_op jit(solution)/shard_map/reshape | solution.py:124
  399.7 1.0 pad.9
  400.7 2.8 copy.244
  403.5 5.9 fusion.12
  409.3 4.7 copy.200
  414.0 42.0 %all_to_all.67 = bf16[666,16,8,16]{0,3,2,1:T(8,128)(2,1)S(1)} all-to-all(bf16[666,16,8,16]{0,3,2,1:T(8,128)(2,1)} %bitcast.685), channel_id=1, replica_groups=mesh['row'=16,'col'=8] {'row'}, dimensions={1} | all-to-all | bytes 5455872 | tf_op jit(solution)/shard_map/all_to_all | solution.py:134
  456.1 3.4 copy.201
  459.5 6.9 %all_to_all.56 = bf16[10656,1,8,16]{0,3,2,1:T(8,128)(2,1)} reshape(bf16[16,666,1,8,16]{1,0,4,3,2:T(8,128)(2,1)} %copy.201) | data formatting | bytes 5455872 | tf_op jit(solution)/shard_map/all_to_all | solution.py:134
  466.4 30.8 %reduce-scatter.5.cloned.1.call-done = bf16[10656,1,1,16]{0,3,2,1:T(8,128)(2,1)} async-done(((bf16[10656,1,8,16]{0,3,2,1:T(8,128)(2,1)}), bf16[10656,1,1,16]{0,3,2,1:T(8,128)(2,1)}) %reduce-scatter.5.cloned.1.call-update) | async-done | bytes 341008 | tf_op jit(solution)/shard_map/reduce_scatter | solution.py:137
  497.1 1.3 reshape_reshape.7
  508.4 0.7 fusion.42
  518.0 0.7 fusion.56
  523.6 0.7 fusion.64
  529.8 0.7 fusion.73
  535.7 1.6 concatenate.21
  537.7 13.0 %concatenate.20 = bf16[2,9417,16]{1,0,2:T(2,128)(2,1)S(1)} concatenate(bf16[2,144,16]{1,0,2:T(2,128)(2,1)S(1)} %slice.2929, bf16[2,1,16]{1,0,2:T(2,128)(2,1)S(1)} %broadcast.227, bf16[2,71,16]{1,0,2:T(2,128)(2,1)} %get-tuple-element.345, bf16[2,2,16]{1,0,2:T(2,128)(2,1)S(1)} %broadcast.228, bf16[2,70,16]{1,0,2:T(2,128)(2,1)} %get-tuple-element.343, ...), dimensions={1} | concatenate | bytes 1205376
  550.7 1.5 pad_maximum_fusion.1
  552.2 3.7 reshape.81
  555.9 3.5 convolution_bitcast_fusion
  559.4 7.1 %fusion.6 = f32[2,16,144,288]{3,2,1,0:T(8,128)S(1)} fusion(f32[145,288,1,1]{1,0,3,2:T(8,128)S(1)} %copy-done.1, f32[2,16,144,145]{2,1,0,3:T(8,128)S(1)} %convolution_bitcast_fusion), kind=kOutput, calls=%fused_computation.8 | convolution fusion | flops 1154580480 | bytes 8148096 | tf_op jit(solution)/shard_map/cktq,qp->cktp/dot_general | solution.py:95
  566.6 0.7 multiply_add_fusion.1
  567.3 5.6 fusion.3
  573.0 6.5 %copy.205 = f32[2,16,144,145]{2,1,0,3:T(8,128)} copy(f32[2,16,144,145]{3,2,1,0:T(8,128)} %fusion.3) | data formatting | bytes 5345280 | tf_op jit(solution)/shard_map/cktp,qp->cktq/dot_general | solution.py:101
  579.5 9.8 %fusion.15 = bf16[2,145,72,16]{2,3,0,1:T(8,128)(2,1)S(1)} fusion(f32[2,16,144,145]{2,1,0,3:T(8,128)} %copy.205, f32[145,72,144,1]{2,1,3,0:T(8,128)} %constant.13), kind=kOutput, calls=%fused_computation.27 | convolution fusion | flops 288979200 | bytes 9354240 | tf_op jit(solution)/shard_map/qlt,cktq->cqlk/dot_general | solution.py:104
  596.1 0.9 concatenate.19
  597.6 14.0 %all_to_all.68 = bf16[8,1332,1,16]{1,3,2,0:T(8,128)(2,1)S(1)} all-to-all(bf16[8,1332,1,16]{1,3,2,0:T(8,128)(2,1)S(1)} %copy.221), channel_id=1, replica_groups=mesh['row'=16,'col'=8] {'col'}, dimensions={0} | all-to-all | bytes 681984 | tf_op jit(solution)/shard_map/all_to_all | solution.py:145
  611.8 0.9 copy.222
  (591 shorter events, 91.0 us)
Async XLA Ops:
  6.5 95.5 %copy-start = (bf16[666,1332]{1,0:T(8,128)(2,1)S(1)}, bf16[666,1332]{1,0:T(8,128)(2,1)}, u32[]{:S(2)}) copy-start(bf16[666,1332]{1,0:T(8,128)(2,1)} %param.11) | copy-start | bytes 5322676
  6.5 188.2 %reduce-scatter.3.cloned.1.call-start = ((), (), s32[]{:S(2)}) async-start(), calls=%async_computation.8 | async-start | bytes 3096576 | tf_op jit(solution)/shard_map/reduce_scatter | solution.py:137
  224.6 20.7 %copy-start.82 = (bf16[2,58,16]{1,0,2:T(2,128)(2,1)}, bf16[2,58,16]{1,0,2:T(2,128)(2,1)S(1)}, u32[]{:S(2)}) copy-start(bf16[2,58,16]{1,0,2:T(2,128)(2,1)S(1)} %broadcast.284) | copy-start | bytes 11140
  224.6 20.7 %copy-start.84 = (bf16[2,59,16]{1,0,2:T(2,128)(2,1)}, bf16[2,59,16]{1,0,2:T(2,128)(2,1)S(1)}, u32[]{:S(2)}) copy-start(bf16[2,59,16]{1,0,2:T(2,128)(2,1)S(1)} %broadcast.285) | copy-start | bytes 11332
  224.6 20.7 %copy-start.86 = (bf16[2,60,16]{1,0,2:T(2,128)(2,1)}, bf16[2,60,16]{1,0,2:T(2,128)(2,1)S(1)}, u32[]{:S(2)}) copy-start(bf16[2,60,16]{1,0,2:T(2,128)(2,1)S(1)} %broadcast.286) | copy-start | bytes 11524
  224.7 20.7 %copy-start.88 = (bf16[2,61,16]{1,0,2:T(2,128)(2,1)}, bf16[2,61,16]{1,0,2:T(2,128)(2,1)S(1)}, u32[]{:S(2)}) copy-start(bf16[2,61,16]{1,0,2:T(2,128)(2,1)S(1)} %broadcast.287) | copy-start | bytes 11716
  232.6 12.7 %copy-start.12 = (bf16[2,23,16]{1,0,2:T(2,128)(2,1)}, bf16[2,23,16]{1,0,2:T(2,128)(2,1)S(1)}, u32[]{:S(2)}) copy-start(bf16[2,23,16]{1,0,2:T(2,128)(2,1)S(1)} %broadcast.249) | copy-start | bytes 4420
  232.7 12.7 %copy-start.14 = (bf16[2,24,16]{1,0,2:T(2,128)(2,1)}, bf16[2,24,16]{1,0,2:T(2,128)(2,1)S(1)}, u32[]{:S(2)}) copy-start(bf16[2,24,16]{1,0,2:T(2,128)(2,1)S(1)} %broadcast.250) | copy-start | bytes 4612
  232.7 12.7 %copy-start.16 = (bf16[2,25,16]{1,0,2:T(2,128)(2,1)}, bf16[2,25,16]{1,0,2:T(2,128)(2,1)S(1)}, u32[]{:S(2)}) copy-start(bf16[2,25,16]{1,0,2:T(2,128)(2,1)S(1)} %broadcast.251) | copy-start | bytes 4804
  232.7 12.7 %copy-start.18 = (bf16[2,26,16]{1,0,2:T(2,128)(2,1)}, bf16[2,26,16]{1,0,2:T(2,128)(2,1)S(1)}, u32[]{:S(2)}) copy-start(bf16[2,26,16]{1,0,2:T(2,128)(2,1)S(1)} %broadcast.252) | copy-start | bytes 4996
  232.7 12.7 %copy-start.20 = (bf16[2,27,16]{1,0,2:T(2,128)(2,1)}, bf16[2,27,16]{1,0,2:T(2,128)(2,1)S(1)}, u32[]{:S(2)}) copy-start(bf16[2,27,16]{1,0,2:T(2,128)(2,1)S(1)} %broadcast.253) | copy-start | bytes 5188
  232.8 12.7 %copy-start.22 = (bf16[2,28,16]{1,0,2:T(2,128)(2,1)}, bf16[2,28,16]{1,0,2:T(2,128)(2,1)S(1)}, u32[]{:S(2)}) copy-start(bf16[2,28,16]{1,0,2:T(2,128)(2,1)S(1)} %broadcast.254) | copy-start | bytes 5380
  232.8 12.6 %copy-start.24 = (bf16[2,29,16]{1,0,2:T(2,128)(2,1)}, bf16[2,29,16]{1,0,2:T(2,128)(2,1)S(1)}, u32[]{:S(2)}) copy-start(bf16[2,29,16]{1,0,2:T(2,128)(2,1)S(1)} %broadcast.255) | copy-start | bytes 5572
  232.8 12.6 %copy-start.26 = (bf16[2,30,16]{1,0,2:T(2,128)(2,1)}, bf16[2,30,16]{1,0,2:T(2,128)(2,1)S(1)}, u32[]{:S(2)}) copy-start(bf16[2,30,16]{1,0,2:T(2,128)(2,1)S(1)} %broadcast.256) | copy-start | bytes 5764
  232.8 12.6 %copy-start.28 = (bf16[2,31,16]{1,0,2:T(2,128)(2,1)}, bf16[2,31,16]{1,0,2:T(2,128)(2,1)S(1)}, u32[]{:S(2)}) copy-start(bf16[2,31,16]{1,0,2:T(2,128)(2,1)S(1)} %broadcast.257) | copy-start | bytes 5956
  232.9 12.6 %copy-start.30 = (bf16[2,32,16]{1,0,2:T(2,128)(2,1)}, bf16[2,32,16]{1,0,2:T(2,128)(2,1)S(1)}, u32[]{:S(2)}) copy-start(bf16[2,32,16]{1,0,2:T(2,128)(2,1)S(1)} %broadcast.258) | copy-start | bytes 6148
  232.9 12.6 %copy-start.32 = (bf16[2,33,16]{1,0,2:T(2,128)(2,1)}, bf16[2,33,16]{1,0,2:T(2,128)(2,1)S(1)}, u32[]{:S(2)}) copy-start(bf16[2,33,16]{1,0,2:T(2,128)(2,1)S(1)} %broadcast.259) | copy-start | bytes 6340
  232.9 12.6 %copy-start.34 = (bf16[2,34,16]{1,0,2:T(2,128)(2,1)}, bf16[2,34,16]{1,0,2:T(2,128)(2,1)S(1)}, u32[]{:S(2)}) copy-start(bf16[2,34,16]{1,0,2:T(2,128)(2,1)S(1)} %broadcast.260) | copy-start | bytes 6532
  232.9 12.6 %copy-start.36 = (bf16[2,35,16]{1,0,2:T(2,128)(2,1)}, bf16[2,35,16]{1,0,2:T(2,128)(2,1)S(1)}, u32[]{:S(2)}) copy-start(bf16[2,35,16]{1,0,2:T(2,128)(2,1)S(1)} %broadcast.261) | copy-start | bytes 6724
  233.0 12.5 %copy-start.38 = (bf16[2,36,16]{1,0,2:T(2,128)(2,1)}, bf16[2,36,16]{1,0,2:T(2,128)(2,1)S(1)}, u32[]{:S(2)}) copy-start(bf16[2,36,16]{1,0,2:T(2,128)(2,1)S(1)} %broadcast.262) | copy-start | bytes 6916
  233.0 12.5 %copy-start.40 = (bf16[2,37,16]{1,0,2:T(2,128)(2,1)}, bf16[2,37,16]{1,0,2:T(2,128)(2,1)S(1)}, u32[]{:S(2)}) copy-start(bf16[2,37,16]{1,0,2:T(2,128)(2,1)S(1)} %broadcast.263) | copy-start | bytes 7108
  233.0 12.5 %copy-start.42 = (bf16[2,38,16]{1,0,2:T(2,128)(2,1)}, bf16[2,38,16]{1,0,2:T(2,128)(2,1)S(1)}, u32[]{:S(2)}) copy-start(bf16[2,38,16]{1,0,2:T(2,128)(2,1)S(1)} %broadcast.264) | copy-start | bytes 7300
  303.9 15.4 %all-to-all-start.2 = ((bf16[8,1332,1,16]{1,3,2,0:T(8,128)(2,1)}), bf16[8,1332,1,16]{1,3,2,0:T(8,128)(2,1)}, u32[]{:S(2)}, u32[]{:S(2)}) async-start(bf16[8,1332,1,16]{1,3,2,0:T(8,128)(2,1)} %copy.197), calls=%async_computation.3 | async-start | bytes 720896 | tf_op jit(solution)/shard_map/all_to_all | solution.py:145
  311.4 185.7 %reduce-scatter.5.cloned.1.call-start = ((), (), s32[]{:S(2)}) async-start(), calls=%async_computation.9 | async-start | bytes 3096576 | tf_op jit(solution)/shard_map/reduce_scatter | solution.py:137
  498.5 37.2 %copy-start.83 = (bf16[2,58,16]{1,0,2:T(2,128)(2,1)S(1)}, bf16[2,58,16]{1,0,2:T(2,128)(2,1)}, u32[]{:S(2)}) copy-start(bf16[2,58,16]{1,0,2:T(2,128)(2,1)} %copy-done.82) | copy-start | bytes 11140
  498.5 37.2 %copy-start.85 = (bf16[2,59,16]{1,0,2:T(2,128)(2,1)S(1)}, bf16[2,59,16]{1,0,2:T(2,128)(2,1)}, u32[]{:S(2)}) copy-start(bf16[2,59,16]{1,0,2:T(2,128)(2,1)} %copy-done.84) | copy-start | bytes 11332
  498.5 37.2 %copy-start.87 = (bf16[2,60,16]{1,0,2:T(2,128)(2,1)S(1)}, bf16[2,60,16]{1,0,2:T(2,128)(2,1)}, u32[]{:S(2)}) copy-start(bf16[2,60,16]{1,0,2:T(2,128)(2,1)} %copy-done.86) | copy-start | bytes 11524
  498.5 37.2 %copy-start.89 = (bf16[2,61,16]{1,0,2:T(2,128)(2,1)S(1)}, bf16[2,61,16]{1,0,2:T(2,128)(2,1)}, u32[]{:S(2)}) copy-start(bf16[2,61,16]{1,0,2:T(2,128)(2,1)} %copy-done.88) | copy-start | bytes 11716
  504.6 32.7 %copy-start.13 = (bf16[2,23,16]{1,0,2:T(2,128)(2,1)S(1)}, bf16[2,23,16]{1,0,2:T(2,128)(2,1)}, u32[]{:S(2)}) copy-start(bf16[2,23,16]{1,0,2:T(2,128)(2,1)} %copy-done.12) | copy-start | bytes 4420
  504.6 32.7 %copy-start.15 = (bf16[2,24,16]{1,0,2:T(2,128)(2,1)S(1)}, bf16[2,24,16]{1,0,2:T(2,128)(2,1)}, u32[]{:S(2)}) copy-start(bf16[2,24,16]{1,0,2:T(2,128)(2,1)} %copy-done.14) | copy-start | bytes 4612
  504.6 32.7 %copy-start.17 = (bf16[2,25,16]{1,0,2:T(2,128)(2,1)S(1)}, bf16[2,25,16]{1,0,2:T(2,128)(2,1)}, u32[]{:S(2)}) copy-start(bf16[2,25,16]{1,0,2:T(2,128)(2,1)} %copy-done.16) | copy-start | bytes 4804
  504.7 32.7 %copy-start.19 = (bf16[2,26,16]{1,0,2:T(2,128)(2,1)S(1)}, bf16[2,26,16]{1,0,2:T(2,128)(2,1)}, u32[]{:S(2)}) copy-start(bf16[2,26,16]{1,0,2:T(2,128)(2,1)} %copy-done.18) | copy-start | bytes 4996
  504.7 32.7 %copy-start.21 = (bf16[2,27,16]{1,0,2:T(2,128)(2,1)S(1)}, bf16[2,27,16]{1,0,2:T(2,128)(2,1)}, u32[]{:S(2)}) copy-start(bf16[2,27,16]{1,0,2:T(2,128)(2,1)} %copy-done.20) | copy-start | bytes 5188
  504.7 32.7 %copy-start.23 = (bf16[2,28,16]{1,0,2:T(2,128)(2,1)S(1)}, bf16[2,28,16]{1,0,2:T(2,128)(2,1)}, u32[]{:S(2)}) copy-start(bf16[2,28,16]{1,0,2:T(2,128)(2,1)} %copy-done.22) | copy-start | bytes 5380
  504.7 32.7 %copy-start.25 = (bf16[2,29,16]{1,0,2:T(2,128)(2,1)S(1)}, bf16[2,29,16]{1,0,2:T(2,128)(2,1)}, u32[]{:S(2)}) copy-start(bf16[2,29,16]{1,0,2:T(2,128)(2,1)} %copy-done.24) | copy-start | bytes 5572
  504.7 32.7 %copy-start.27 = (bf16[2,30,16]{1,0,2:T(2,128)(2,1)S(1)}, bf16[2,30,16]{1,0,2:T(2,128)(2,1)}, u32[]{:S(2)}) copy-start(bf16[2,30,16]{1,0,2:T(2,128)(2,1)} %copy-done.26) | copy-start | bytes 5764
  504.7 32.7 %copy-start.29 = (bf16[2,31,16]{1,0,2:T(2,128)(2,1)S(1)}, bf16[2,31,16]{1,0,2:T(2,128)(2,1)}, u32[]{:S(2)}) copy-start(bf16[2,31,16]{1,0,2:T(2,128)(2,1)} %copy-done.28) | copy-start | bytes 5956
  504.7 32.7 %copy-start.31 = (bf16[2,32,16]{1,0,2:T(2,128)(2,1)S(1)}, bf16[2,32,16]{1,0,2:T(2,128)(2,1)}, u32[]{:S(2)}) copy-start(bf16[2,32,16]{1,0,2:T(2,128)(2,1)} %copy-done.30) | copy-start | bytes 6148
  504.7 32.7 %copy-start.33 = (bf16[2,33,16]{1,0,2:T(2,128)(2,1)S(1)}, bf16[2,33,16]{1,0,2:T(2,128)(2,1)}, u32[]{:S(2)}) copy-start(bf16[2,33,16]{1,0,2:T(2,128)(2,1)} %copy-done.32) | copy-start | bytes 6340
  504.7 32.7 %copy-start.35 = (bf16[2,34,16]{1,0,2:T(2,128)(2,1)S(1)}, bf16[2,34,16]{1,0,2:T(2,128)(2,1)}, u32[]{:S(2)}) copy-start(bf16[2,34,16]{1,0,2:T(2,128)(2,1)} %copy-done.34) | copy-start | bytes 6532
  504.7 32.7 %copy-start.37 = (bf16[2,35,16]{1,0,2:T(2,128)(2,1)S(1)}, bf16[2,35,16]{1,0,2:T(2,128)(2,1)}, u32[]{:S(2)}) copy-start(bf16[2,35,16]{1,0,2:T(2,128)(2,1)} %copy-done.36) | copy-start | bytes 6724
  504.7 32.7 %copy-start.39 = (bf16[2,36,16]{1,0,2:T(2,128)(2,1)S(1)}, bf16[2,36,16]{1,0,2:T(2,128)(2,1)}, u32[]{:S(2)}) copy-start(bf16[2,36,16]{1,0,2:T(2,128)(2,1)} %copy-done.38) | copy-start | bytes 6916
  504.8 32.7 %copy-start.41 = (bf16[2,37,16]{1,0,2:T(2,128)(2,1)S(1)}, bf16[2,37,16]{1,0,2:T(2,128)(2,1)}, u32[]{:S(2)}) copy-start(bf16[2,37,16]{1,0,2:T(2,128)(2,1)} %copy-done.40) | copy-start | bytes 7108
  504.8 32.7 %copy-start.43 = (bf16[2,38,16]{1,0,2:T(2,128)(2,1)S(1)}, bf16[2,38,16]{1,0,2:T(2,128)(2,1)}, u32[]{:S(2)}) copy-start(bf16[2,38,16]{1,0,2:T(2,128)(2,1)} %copy-done.42) | copy-start | bytes 7300
  504.8 32.7 %copy-start.45 = (bf16[2,39,16]{1,0,2:T(2,128)(2,1)S(1)}, bf16[2,39,16]{1,0,2:T(2,128)(2,1)}, u32[]{:S(2)}) copy-start(bf16[2,39,16]{1,0,2:T(2,128)(2,1)} %copy-done.44) | copy-start | bytes 7492
  504.8 32.7 %copy-start.47 = (bf16[2,40,16]{1,0,2:T(2,128)(2,1)S(1)}, bf16[2,40,16]{1,0,2:T(2,128)(2,1)}, u32[]{:S(2)}) copy-start(bf16[2,40,16]{1,0,2:T(2,128)(2,1)} %copy-done.46) | copy-start | bytes 7684
  504.8 32.7 %copy-start.49 = (bf16[2,41,16]{1,0,2:T(2,128)(2,1)S(1)}, bf16[2,41,16]{1,0,2:T(2,128)(2,1)}, u32[]{:S(2)}) copy-start(bf16[2,41,16]{1,0,2:T(2,128)(2,1)} %copy-done.48) | copy-start | bytes 7876
  504.8 32.7 %copy-start.51 = (bf16[2,42,16]{1,0,2:T(2,128)(2,1)S(1)}, bf16[2,42,16]{1,0,2:T(2,128)(2,1)}, u32[]{:S(2)}) copy-start(bf16[2,42,16]{1,0,2:T(2,128)(2,1)} %copy-done.50) | copy-start | bytes 8068
  504.8 32.7 %copy-start.53 = (bf16[2,43,16]{1,0,2:T(2,128)(2,1)S(1)}, bf16[2,43,16]{1,0,2:T(2,128)(2,1)}, u32[]{:S(2)}) copy-start(bf16[2,43,16]{1,0,2:T(2,128)(2,1)} %copy-done.52) | copy-start | bytes 8260
  504.8 32.7 %copy-start.55 = (bf16[2,44,16]{1,0,2:T(2,128)(2,1)S(1)}, bf16[2,44,16]{1,0,2:T(2,128)(2,1)}, u32[]{:S(2)}) copy-start(bf16[2,44,16]{1,0,2:T(2,128)(2,1)} %copy-done.54) | copy-start | bytes 8452
  504.8 32.7 %copy-start.57 = (bf16[2,45,16]{1,0,2:T(2,128)(2,1)S(1)}, bf16[2,45,16]{1,0,2:T(2,128)(2,1)}, u32[]{:S(2)}) copy-start(bf16[2,45,16]{1,0,2:T(2,128)(2,1)} %copy-done.56) | copy-start | bytes 8644
  504.8 32.7 %copy-start.59 = (bf16[2,46,16]{1,0,2:T(2,128)(2,1)S(1)}, bf16[2,46,16]{1,0,2:T(2,128)(2,1)}, u32[]{:S(2)}) copy-start(bf16[2,46,16]{1,0,2:T(2,128)(2,1)} %copy-done.58) | copy-start | bytes 8836
  504.9 32.7 %copy-start.61 = (bf16[2,47,16]{1,0,2:T(2,128)(2,1)S(1)}, bf16[2,47,16]{1,0,2:T(2,128)(2,1)}, u32[]{:S(2)}) copy-start(bf16[2,47,16]{1,0,2:T(2,128)(2,1)} %copy-done.60) | copy-start | bytes 9028
  504.9 32.7 %copy-start.63 = (bf16[2,48,16]{1,0,2:T(2,128)(2,1)S(1)}, bf16[2,48,16]{1,0,2:T(2,128)(2,1)}, u32[]{:S(2)}) copy-start(bf16[2,48,16]{1,0,2:T(2,128)(2,1)} %copy-done.62) | copy-start | bytes 9220
  504.9 32.7 %copy-start.65 = (bf16[2,49,16]{1,0,2:T(2,128)(2,1)S(1)}, bf16[2,49,16]{1,0,2:T(2,128)(2,1)}, u32[]{:S(2)}) copy-start(bf16[2,49,16]{1,0,2:T(2,128)(2,1)} %copy-done.64) | copy-start | bytes 9412
  504.9 32.7 %copy-start.67 = (bf16[2,50,16]{1,0,2:T(2,128)(2,1)S(1)}, bf16[2,50,16]{1,0,2:T(2,128)(2,1)}, u32[]{:S(2)}) copy-start(bf16[2,50,16]{1,0,2:T(2,128)(2,1)} %copy-done.66) | copy-start | bytes 9604
  504.9 32.7 %copy-start.69 = (bf16[2,51,16]{1,0,2:T(2,128)(2,1)S(1)}, bf16[2,51,16]{1,0,2:T(2,128)(2,1)}, u32[]{:S(2)}) copy-start(bf16[2,51,16]{1,0,2:T(2,128)(2,1)} %copy-done.68) | copy-start | bytes 9796
  504.9 32.7 %copy-start.71 = (bf16[2,52,16]{1,0,2:T(2,128)(2,1)S(1)}, bf16[2,52,16]{1,0,2:T(2,128)(2,1)}, u32[]{:S(2)}) copy-start(bf16[2,52,16]{1,0,2:T(2,128)(2,1)} %copy-done.70) | copy-start | bytes 9988
  504.9 32.7 %copy-start.73 = (bf16[2,53,16]{1,0,2:T(2,128)(2,1)S(1)}, bf16[2,53,16]{1,0,2:T(2,128)(2,1)}, u32[]{:S(2)}) copy-start(bf16[2,53,16]{1,0,2:T(2,128)(2,1)} %copy-done.72) | copy-start | bytes 10180
  504.9 32.7 %copy-start.75 = (bf16[2,54,16]{1,0,2:T(2,128)(2,1)S(1)}, bf16[2,54,16]{1,0,2:T(2,128)(2,1)}, u32[]{:S(2)}) copy-start(bf16[2,54,16]{1,0,2:T(2,128)(2,1)} %copy-done.74) | copy-start | bytes 10372
  504.9 32.7 %copy-start.77 = (bf16[2,55,16]{1,0,2:T(2,128)(2,1)S(1)}, bf16[2,55,16]{1,0,2:T(2,128)(2,1)}, u32[]{:S(2)}) copy-start(bf16[2,55,16]{1,0,2:T(2,128)(2,1)} %copy-done.76) | copy-start | bytes 10564
  504.9 32.7 %copy-start.79 = (bf16[2,56,16]{1,0,2:T(2,128)(2,1)S(1)}, bf16[2,56,16]{1,0,2:T(2,128)(2,1)}, u32[]{:S(2)}) copy-start(bf16[2,56,16]{1,0,2:T(2,128)(2,1)} %copy-done.78) | copy-start | bytes 10756
  505.0 32.7 %copy-start.81 = (bf16[2,57,16]{1,0,2:T(2,128)(2,1)S(1)}, bf16[2,57,16]{1,0,2:T(2,128)(2,1)}, u32[]{:S(2)}) copy-start(bf16[2,57,16]{1,0,2:T(2,128)(2,1)} %copy-done.80) | copy-start | bytes 10948
  597.6 14.1 %copy-start.3 = (bf16[1332,128]{0,1:T(8,128)(2,1)S(1)}, bf16[1332,128]{0,1:T(8,128)(2,1)}, u32[]{:S(2)}) copy-start(bf16[1332,128]{0,1:T(8,128)(2,1)} %copy-done.2) | copy-start | bytes 1022980
  (30 other events, 301.4 us)
Sparse Core Ops, SparseCore 0:
  161.1 33.6 reduce-scatter.2
  466.5 30.6 reduce-scatter.4
